TPU v7x, 32 devices: a whole 2x2x4 slice. The times are simulated.
32 devices in a mesh: dp: 16 (over z, y, x), mp: 2 (over core).
Axes of the slice: x: 2, y: 2, z: 4, core: 2. Of those that a mesh axis runs over, the one named last changes fastest.
Arguments:
- train_in: bfloat16 [1024, 64, 16], P('dp'), may hold values from -6 to 6
- train_out_grad: bfloat16 [1024, 64, 1024], P('dp', None, 'mp'), may hold values from -6 to 6
- query_in: bfloat16 [1024, 64, 16], P('dp'), may hold values from -6 to 6
- query_out_grad: bfloat16 [1024, 64, 1024], P('dp', None, 'mp'), may hold values from -6 to 6
- query_owner: int32 [1024, 1], P('dp'), may hold values from 0 to 15; in each aligned block of 64 rows (0 to 63, 64 to 127, ...) at most 8 rows name the same one
- sketch_seed: int32 [1], replicated, may hold values from 0 to 1073741823
Outputs:
- kernel: float32 [1024, 1024], P('mp', 'dp')
- owner_scores: float32 [16, 16, 8, 64], P('dp')
Inputs may be any that keep to these rules, and one draw needn't show every extreme that they name: `query_owner`: within the queries of one device (aligned blocks of 64), one owner is named at most 8 times, a bound that some block reaches in every draw.
All inputs are finite; a program needn't handle non-finite values.
Results may differ from a plain program's by a relative error of at most 0.0041.
Values may be sent and summed in bfloat16 or wider, within the bound.
A program may use at most 64 MiB of HBM per device.

v0:
```python
import functools
import math

import jax
import jax.numpy as jnp
from jax import lax
from jax.experimental import pallas as pl
from jax.experimental.pallas import tpu as pltpu
from jax.sharding import PartitionSpec as P

VW = 1024
R = 16
K = 8192
L = 64
BLOCK = 64
ROWS = 16
AHEAD = 2

hash_factor = 73244475


def as_word(value):
    value &= 0xFFFFFFFF
    return value - (1 << 32) if value >= 1 << 31 else value


last_factor = as_word((hash_factor + 65536) << 15)


def local_grads(inputs, out_grads):
    return jnp.einsum("ntr,ntj->rnj", inputs, out_grads, preferred_element_type=jnp.float32).astype(
        jnp.bfloat16
    )


MESH = pl.DeviceIdType.MESH


def trak_kernel(
    n_mp,
    early,
    seed_ref,
    train_ref,
    query_ref,
    placing_ref,
    select_ref,
    gram_ref,
    scores_ref,
    held,
    table,
    acc,
    blocks_ref,
    qout,
    routed_ref,
    wide,
    keep,
    xout,
    xin,
    gout,
    gin,
    parts,
    rank_sems,
    core_sems,
    query_sems,
    feat_sems,
    fwd_sems,
    pair_sems,
    gram_sems,
    score_sems,
):
    n_pairs, pair_rows, cols = blocks_ref.shape
    n_dp = routed_ref.shape[0]
    n_tiles, _, tile_cols = table.shape
    per_tile = tile_cols // cols
    width = train_ref.shape[2]
    n_splits = placing_ref.shape[0]
    split_ranks = R // n_splits
    examples = pair_rows // 2
    n_rows = n_pairs * pair_rows // n_mp
    dp = lax.axis_index("dp")
    mp = lax.axis_index("mp")
    pair = dp // 2
    side = dp % 2
    mate = pair * 2 + 1 - side
    others = n_pairs - 1

    def later(i):
        return lax.rem(pair + 1 + i, n_pairs)

    def core(step):
        return lax.rem(mp + step, n_mp)

    def rank_copy(rank, rows):
        return pltpu.make_async_remote_copy(
            src_ref=train_ref.at[rank],
            dst_ref=held.at[mp, rank, rows],
            send_sem=rank_sems.at[0, rank],
            recv_sem=rank_sems.at[1, rank],
            device_id=(mate, mp),
            device_id_type=MESH,
        )

    def core_copy(step, part, rank):
        return pltpu.make_async_remote_copy(
            src_ref=held.at[part, rank],
            dst_ref=held.at[part, rank],
            send_sem=core_sems.at[0, step - 1, rank],
            recv_sem=core_sems.at[1, step - 1, rank],
            device_id=(dp, core(step)),
            device_id_type=MESH,
        )

    def query_copy(target, source):
        return pltpu.make_async_remote_copy(
            src_ref=qout.at[target],
            dst_ref=routed_ref.at[source],
            send_sem=query_sems.at[0, target],
            recv_sem=query_sems.at[1, source],
            device_id=(target, mp),
            device_id_type=MESH,
        )

    def feat_copy(target, source):
        return pltpu.make_async_remote_copy(
            src_ref=blocks_ref.at[target],
            dst_ref=wide.at[mp, source],
            send_sem=feat_sems.at[0, target],
            recv_sem=feat_sems.at[1, source],
            device_id=(target * 2 + side, mp),
            device_id_type=MESH,
        )

    def fwd_copy(step, part, source):
        return pltpu.make_async_remote_copy(
            src_ref=wide.at[part, source],
            dst_ref=wide.at[part, source],
            send_sem=fwd_sems.at[0, step - 1, source],
            recv_sem=fwd_sems.at[1, step - 1, source],
            device_id=(dp, core(step)),
            device_id_type=MESH,
        )

    def pair_copy(target):
        return pltpu.make_async_remote_copy(
            src_ref=xout.at[target],
            dst_ref=xin.at[target],
            send_sem=pair_sems.at[0, target],
            recv_sem=pair_sems.at[1, target],
            device_id=(mate, mp),
            device_id_type=MESH,
        )

    def gram_copy(target, source):
        return pltpu.make_async_remote_copy(
            src_ref=gout.at[target],
            dst_ref=gin.at[source],
            send_sem=gram_sems.at[0, target],
            recv_sem=gram_sems.at[1, source],
            device_id=(target * 2 + side, mp),
            device_id_type=MESH,
        )

    def score_copy(step, part):
        return pltpu.make_async_remote_copy(
            src_ref=parts.at[part],
            dst_ref=parts.at[part],
            send_sem=score_sems.at[0, step - 1],
            recv_sem=score_sems.at[1, step - 1],
            device_id=(dp, core(step)),
            device_id_type=MESH,
        )

    barrier = pltpu.get_barrier_semaphore()

    @pl.loop(1, n_dp)
    def _(i):
        pl.semaphore_signal(
            barrier, inc=1, device_id=(lax.rem(dp + i, n_dp), mp), device_id_type=MESH
        )

    for step in range(1, n_mp):
        pl.semaphore_signal(barrier, inc=1, device_id=(dp, core(step)), device_id_type=MESH)
    pl.semaphore_wait(barrier, n_dp - 1 + n_mp - 1)

    @pl.loop(0, R)
    def _(rank):
        rank_copy(rank, side).start()
        held[mp, rank, side] = train_ref[rank]

    @pl.loop(0, split_ranks)
    def _(i):
        placed = None
        for split in range(n_splits):
            term = jnp.dot(
                placing_ref[split],
                query_ref[split * split_ranks + i],
                preferred_element_type=jnp.float32,
            )
            placed = term if placed is None else placed + term
        part = pl.ds(pl.multiple_of(i * width, width), width)
        qout[:, :, part] = placed.astype(qout.dtype).reshape(n_dp, ROWS, width)

    @pl.loop(1, n_dp)
    def _(i):
        query_copy(lax.rem(dp + i, n_dp), dp).start()

    routed_ref[dp] = qout[dp]

    seed = seed_ref[0]
    upper = lax.shift_right_logical(seed, jnp.int32(K.bit_length() - 1))
    spread = as_word(K * hash_factor)
    place = side * n_mp + mp
    inner = lax.broadcasted_iota(jnp.int32, (BLOCK, tile_cols), 0)
    outer = lax.broadcasted_iota(jnp.int32, (BLOCK, tile_cols), 1)

    @pl.loop(0, n_tiles)
    def _(tile):
        column = (place * n_tiles + tile) * tile_cols + outer
        table[tile] = (inner ^ (upper & (BLOCK - 1))) * spread + (
            column ^ (seed & (K - 1))
        ) * hash_factor
        acc[tile] = jnp.zeros(acc.shape[1:], jnp.float32)

    def signs(rank, part, tile):
        pieces = []
        for start in range(0, width, BLOCK):
            base = rank * VW + part * width + start
            mixing = table[tile] + (base ^ (upper & ~(BLOCK - 1))) * spread
            mixing = mixing ^ lax.shift_right_logical(mixing, jnp.full_like(mixing, 16))
            mixing = mixing * last_factor
            pieces.append(
                jnp.where(mixing < 0, jnp.float32(-1), jnp.float32(1)).astype(jnp.bfloat16)
            )
        return jnp.concatenate(pieces, axis=0)

    def project(rank, tile):
        total = None
        for part in range(n_mp):
            term = jnp.dot(
                held[part, rank].reshape(pair_rows, width),
                signs(rank, part, tile),
                preferred_element_type=jnp.float32,
            )
            total = term if total is None else total + term
        acc[tile] += total

    def forward(rank):
        rank_copy(rank, 1 - side).wait_recv()
        for step in range(1, n_mp):
            core_copy(step, mp, rank).start()

    def arrived(rank):
        for step in range(1, n_mp):
            core_copy(step, core(n_mp - step), rank).wait_recv()

    for rank in range(AHEAD):
        forward(rank)

    @pl.loop(0, early)
    def _(rank):
        forward(rank + AHEAD)
        arrived(rank)

        @pl.loop(0, n_tiles)
        def _(tile):
            project(rank, tile)

    @pl.loop(early + AHEAD, R)
    def _(rank):
        forward(rank)

    @pl.loop(early, R)
    def _(rank):
        arrived(rank)

    @pl.loop(0, n_tiles)
    def _(i):
        tile = lax.rem(lax.div(pair, per_tile) + 1 + i, n_tiles)

        @pl.loop(early, R)
        def _(rank):
            project(rank, tile)

        made = (acc[tile] * (1.0 / math.sqrt(L * R * VW))).astype(blocks_ref.dtype)
        for j in range(per_tile):
            target = tile * per_tile + j
            blocks_ref[target] = made[:, j * cols : (j + 1) * cols]

            @pl.when(target != pair)
            def _():
                feat_copy(target, pair).start()

    wide[mp, pair] = blocks_ref[pair]
    for step in range(1, n_mp):
        fwd_copy(step, mp, pair).start()

    @pl.loop(0, others)
    def _(i):
        source = lax.rem(pair + others - i, n_pairs)
        feat_copy(source, source).wait_recv()
        for step in range(1, n_mp):
            fwd_copy(step, mp, source).start()

    @pl.loop(0, n_pairs)
    def _(source):
        for step in range(1, n_mp):
            fwd_copy(step, core(n_mp - step), source).wait_recv()

    row_pairs = n_pairs // n_mp
    row_part = pl.ds(mp * row_pairs, row_pairs)

    @pl.loop(0, n_pairs)
    def _(i):
        target = later(i)
        total = None
        for part in range(n_mp):
            term = lax.dot_general(
                wide[part, target],
                wide[part, row_part].reshape(n_rows, -1),
                (((1,), (1,)), ((), ())),
                preferred_element_type=jnp.float32,
            )
            total = term if total is None else total + term
        keep[target] = total.reshape(2, examples, n_rows)
        xout[target] = keep[target, 1 - side].astype(xout.dtype)
        pair_copy(target).start()

    @pl.loop(0, others)
    def _(i):
        target = later(i)
        pair_copy(target).wait_recv()
        gout[target] = (keep[target, side] + xin[target].astype(jnp.float32)).astype(gout.dtype)
        gram_copy(target, pair).start()

    @pl.loop(1, n_dp)
    def _(i):
        source = lax.rem(dp + n_dp - i, n_dp)
        query_copy(source, source).wait_recv()

    parts[mp] = jnp.zeros(parts.shape[1:], jnp.float32)

    @pl.loop(0, split_ranks)
    def _(i):
        part = pl.ds(pl.multiple_of(i * width, width), width)
        rows = routed_ref[:, :, part].reshape(n_dp * ROWS, width)
        for split in range(n_splits):
            parts[mp] += select_ref[split] * lax.dot_general(
                rows,
                train_ref[split * split_ranks + i],
                (((1,), (1,)), ((), ())),
                preferred_element_type=jnp.float32,
            )

    for step in range(1, n_mp):
        score_copy(step, mp).start()

    pair_copy(pair).wait_recv()
    gram_ref[...] = keep[pair, side] + xin[pair].astype(jnp.float32)

    for step in range(1, n_mp):
        score_copy(step, core(n_mp - step)).wait_recv()
    summed = parts[0]
    for part in range(1, n_mp):
        summed = summed + parts[part]
    scores_ref[...] = summed * (1.0 / (L * math.sqrt(R * VW)))

    @pl.loop(0, others)
    def _(i):
        source = lax.rem(pair + others - i, n_pairs)
        gram_copy(source, source).wait_recv()
        gram_ref[...] += gin[source].astype(jnp.float32)

    gram_ref[...] = gram_ref[...] * (1.0 / math.sqrt(K))

    @pl.loop(0, others)
    def _(i):
        feat_copy(later(i), pair).wait_send()
        gram_copy(later(i), pair).wait_send()

    @pl.loop(0, n_pairs)
    def _(source):
        pair_copy(source).wait_send()
        for step in range(1, n_mp):
            fwd_copy(step, mp, source).wait_send()

    for step in range(1, n_mp):
        score_copy(step, mp).wait_send()

    @pl.loop(0, R)
    def _(rank):
        rank_copy(rank, side).wait_send()
        for step in range(1, n_mp):
            core_copy(step, mp, rank).wait_send()

    @pl.loop(1, n_dp)
    def _(i):
        query_copy(lax.rem(dp + i, n_dp), dp).wait_send()


def trak(seed, train, query, placing, select, n_dp, n_mp):
    n_pairs = n_dp // 2
    examples, width = train.shape[1:]
    n_cols = K // (2 * n_mp)
    cols = n_cols // n_pairs
    tile_cols = max(cols, min(256, n_cols))
    n_tiles = n_cols // tile_cols
    n_rows = n_dp * examples // n_mp
    sums = (n_pairs, examples, n_rows)
    blocks = (n_pairs, 2 * examples, cols)
    queries = (n_dp, ROWS, R // placing.shape[0] * width)
    vmem = pl.BlockSpec(memory_space=pltpu.VMEM)
    return pl.pallas_call(
        functools.partial(trak_kernel, n_mp, R * 3 // 4),
        out_shape=(
            jax.ShapeDtypeStruct((examples, n_rows), jnp.float32),
            jax.ShapeDtypeStruct((n_dp * ROWS, examples), jnp.float32),
        ),
        in_specs=[pl.BlockSpec(memory_space=pltpu.SMEM)] + [vmem] * 4,
        out_specs=(vmem, vmem),
        scratch_shapes=[
            pltpu.VMEM((n_mp, R, 2, examples, width), jnp.bfloat16),
            pltpu.VMEM((n_tiles, BLOCK, tile_cols), jnp.int32),
            pltpu.VMEM((n_tiles, 2 * examples, tile_cols), jnp.float32),
            pltpu.VMEM(blocks, jnp.bfloat16),
            pltpu.VMEM(queries, jnp.bfloat16),
            pltpu.VMEM(queries, jnp.bfloat16),
            pltpu.VMEM((n_mp,) + blocks, jnp.bfloat16),
            pltpu.VMEM((n_pairs, 2, examples, n_rows), jnp.float32),
            pltpu.VMEM(sums, jnp.bfloat16),
            pltpu.VMEM(sums, jnp.bfloat16),
            pltpu.VMEM(sums, jnp.bfloat16),
            pltpu.VMEM(sums, jnp.bfloat16),
            pltpu.VMEM((n_mp, n_dp * ROWS, examples), jnp.float32),
            pltpu.SemaphoreType.DMA((2, R)),
            pltpu.SemaphoreType.DMA((2, n_mp - 1, R)),
            pltpu.SemaphoreType.DMA((2, n_dp)),
            pltpu.SemaphoreType.DMA((2, n_pairs)),
            pltpu.SemaphoreType.DMA((2, n_mp - 1, n_pairs)),
            pltpu.SemaphoreType.DMA((2, n_pairs)),
            pltpu.SemaphoreType.DMA((2, n_pairs)),
            pltpu.SemaphoreType.DMA((2, n_mp - 1)),
        ],
        compiler_params=pltpu.CompilerParams(
            collective_id=0, has_side_effects=True, vmem_limit_bytes=48 * 2**20
        ),
        name="trak",
    )(seed, train, query, placing, select)


def shards(train_in, train_out_grad, query_in, query_out_grad, query_owner, sketch_seed):
    n_mp = lax.axis_size("mp")
    n_dp = lax.axis_size("dp")
    train_grads = local_grads(train_in, train_out_grad)
    query_grads = local_grads(query_in, query_out_grad)
    _, queries, _ = query_grads.shape
    examples = train_grads.shape[1]
    capacity = 2 * queries // n_dp
    n_splits = ROWS // capacity

    with jax.named_scope("placing"):
        owners = query_owner[:, 0]
        later_index = lax.broadcasted_iota(jnp.int32, (queries, queries), 0)
        earlier = (owners[:, None] == owners[None, :]) & (
            lax.broadcasted_iota(jnp.int32, (queries, queries), 1) < later_index
        )
        slot_rank = jnp.sum(earlier.astype(jnp.int32), axis=1)
        target = owners * ROWS + slot_rank
        shape = (n_splits, n_dp * ROWS, queries)
        split_ids = lax.broadcasted_iota(jnp.int32, shape, 0)
        row_ids = lax.broadcasted_iota(jnp.int32, shape, 1)
        placing = (row_ids == target[None, None, :] + split_ids * capacity).astype(jnp.bfloat16)
        shape = (n_splits, n_dp * ROWS, examples)
        split_ids = lax.broadcasted_iota(jnp.int32, shape, 0)
        row_ids = lax.broadcasted_iota(jnp.int32, shape, 1)
        select = (row_ids % ROWS // capacity == split_ids).astype(jnp.float32)

    gram, scores = trak(sketch_seed, train_grads, query_grads, placing, select, n_dp, n_mp)
    scores = jnp.sum(scores.reshape(n_dp, n_splits, capacity, examples), axis=1)
    return (gram.T, scores[None])


def solution(mesh):
    return jax.shard_map(
        shards,
        mesh=mesh,
        in_specs=(
            P("dp", None, None),
            P("dp", None, "mp"),
            P("dp", None, None),
            P("dp", None, "mp"),
            P("dp", None),
            P(),
        ),
        out_specs=(P("mp", "dp"), P("dp", None, None, None)),
        check_vma=False,
    )
```

profile of v0, /device:TPU:15, one launch (start us, length us, event | category | flops | bytes accessed | tf_op | source)
XLA Modules:
  0.0 98.0 jit_solution(8149075318151261281)
XLA Ops:
  0.6 0.0 copy-start
  0.6 0.0 copy-start.2
  0.7 0.0 copy-start.1
  1.5 0.1 copy-done
  1.6 3.3 %fusion.12 = bf16[64,512,16]{1,2,0:T(8,128)(2,1)S(1)} fusion(bf16[64,64,16]{1,2,0:T(8,128)(2,1)S(1)} %copy-done, bf16[64,64,512]{2,1,0:T(8,128)(2,1)} %param.7), kind=kOutput, calls=%fused_computation.28 | convolution fusion | flops 67108864 | bytes 5373952 | tf_op jit(solution)/shard_map/ntr,ntj->rnj/dot_general | solution.py:31
  4.9 0.0 copy-done.2
  4.9 0.0 copy-done.1
  4.9 0.0 copy-start.3
  5.0 0.7 fusion.13
  5.6 1.2 %fusion = (bf16[16,64,512]{2,1,0:T(8,128)(2,1)S(1)}, bf16[16,64,512]{2,1,0:T(8,128)(2,1)S(1)}) fusion(bf16[64,512,16]{1,2,0:T(8,128)(2,1)S(1)} %fusion.12, bf16[64,512,16]{1,2,0:T(8,128)(2,1)S(1)} %fusion.13), kind=kLoop, calls=%fused_computation.2 | loop fusion | bytes 4194304 | tf_op jit(solution)/shard_map/convert_element_type | solution.py:31
  6.8 0.0 copy-done.3
  6.8 0.2 convert_reduce_fusion
  7.0 0.1 fusion.9.placing_ref
  7.1 0.2 fusion.7.select_ref
  7.3 89.4 %trak.1 = (f32[64,512]{1,0:T(8,128)S(1)}, f32[256,64]{1,0:T(8,128)S(1)}) custom-call(s32[1]{0:T(128)S(6)} %copy.19.seed_ref, bf16[16,64,512]{2,1,0:T(8,128)(2,1)S(1)} %get-tuple-element.8.train_ref, bf16[16,64,512]{2,1,0:T(8,128)(2,1)S(1)} %get-tuple-element.9.query_ref, bf16[2,256,64]{2,1,0:T(8,128)(2,1)S(1)} %fusion.9.placing_ref, ...), custom_call_target="tpu_custom_call" | custom-call | tf_op jit(solution)/shard_map/trak/pallas_call | solution.py:412
  96.7 0.6 reduce_sum.19
  97.4 0.7 copy.20
  (4 shorter events, 0.0 us)
Async XLA Ops:
  0.6 1.0 copy-start
  0.6 4.3 %copy-start.2 = (bf16[64,64,16]{1,2,0:T(8,128)(2,1)S(1)}, bf16[64,64,16]{1,2,0:T(8,128)(2,1)}, u32[]{:S(2)}) copy-start(bf16[64,64,16]{1,2,0:T(8,128)(2,1)} %param.8) | copy-start | bytes 393220
  0.7 4.3 %copy-start.1 = (bf16[64,64,512]{2,1,0:T(8,128)(2,1)S(1)}, bf16[64,64,512]{2,1,0:T(8,128)(2,1)}, u32[]{:S(2)}) copy-start(bf16[64,64,512]{2,1,0:T(8,128)(2,1)} %param.9) | copy-start | bytes 12582916
  4.9 1.9 %copy-start.3 = (s32[64,1]{0,1:T(1,128)S(1)}, s32[64,1]{0,1:T(1,128)}, u32[]{:S(2)}) copy-start(s32[64,1]{0,1:T(1,128)} %param.10) | copy-start | bytes 772
where the time goes:
time: 99.2 us; the launch traced here: 98 us
  Pallas kernels  89.4 us (90%)
  matrix products  3.99 us (4%)
  local copies, waits for them, and re-layouts  1.97 us (2%)
  between operations  1.55 us (2%)
  other arithmetic  1.12 us (1%)
    pallas_call x1, Pallas kernels, trak(): pl.pallas_call(functools.partial(trak_kernel, n_mp, R * 3 // 4), out_shap...  89.4 us
    dot_general x2, matrix products, local_grads(): jnp.einsum('ntr,ntj->rnj', inputs, out_grads, preferred_element_type=jnp....  3.99 us

commit v1 on v0

--- a/solution.py
+++ b/solution.py
@@ -200,9 +200,7 @@
         part = pl.ds(pl.multiple_of(i * width, width), width)
         qout[:, :, part] = placed.astype(qout.dtype).reshape(n_dp, ROWS, width)
 
-    @pl.loop(1, n_dp)
-    def _(i):
-        query_copy(lax.rem(dp + i, n_dp), dp).start()
+    stride = next(i for i in (5, 3, 7, 1) if math.gcd(i, n_dp) == 1)
 
     routed_ref[dp] = qout[dp]
 
@@ -260,6 +258,10 @@
     def _(rank):
         forward(rank + AHEAD)
         arrived(rank)
+
+        @pl.loop(1 + rank * (n_dp - 1) // early, 1 + (rank + 1) * (n_dp - 1) // early)
+        def _(i):
+            query_copy(lax.rem(dp + i * stride, n_dp), dp).start()
 
         @pl.loop(0, n_tiles)
         def _(tile):

time: 99.2 us -> 100 us (level); the launches traced: 98 us -> 100 us
  Pallas kernels: 89.4 us -> 91.6 us
    pallas_call x1, Pallas kernels: 89.4 us -> 91.6 us  [trak(): pl.pallas_call(functools.partial(trak_kernel, n_mp, R * 3 // 4), out_shap...]
where the time goes in v1:
time: 100 us
  Pallas kernels  91.6 us (92%)
  matrix products  3.99 us (4%)
  local copies, waits for them, and re-layouts  1.97 us (2%)
  between operations  1.55 us (2%)
  other arithmetic  1.12 us (1%)
    pallas_call x1, Pallas kernels, trak(): pl.pallas_call(functools.partial(trak_kernel, n_mp, R * 3 // 4), out_shap...  91.6 us
    dot_general x2, matrix products, local_grads(): jnp.einsum('ntr,ntj->rnj', inputs, out_grads, preferred_element_type=jnp....  3.99 us

profile of v1, /device:TPU:15, one launch (start us, length us, event | category | flops | bytes accessed | tf_op | source)
XLA Modules:
  0.0 100.2 jit_solution(17477711970152052464)
XLA Ops:
  0.6 0.0 copy-start
  0.6 0.0 copy-start.2
  0.7 0.0 copy-start.1
  1.5 0.1 copy-done
  1.6 3.3 %fusion.12 = bf16[64,512,16]{1,2,0:T(8,128)(2,1)S(1)} fusion(bf16[64,64,16]{1,2,0:T(8,128)(2,1)S(1)} %copy-done, bf16[64,64,512]{2,1,0:T(8,128)(2,1)} %param.7), kind=kOutput, calls=%fused_computation.28 | convolution fusion | flops 67108864 | bytes 5373952 | tf_op jit(solution)/shard_map/ntr,ntj->rnj/dot_general | solution.py:31
  4.9 0.0 copy-done.2
  4.9 0.0 copy-done.1
  4.9 0.0 copy-start.3
  5.0 0.7 fusion.13
  5.6 1.2 %fusion = (bf16[16,64,512]{2,1,0:T(8,128)(2,1)S(1)}, bf16[16,64,512]{2,1,0:T(8,128)(2,1)S(1)}) fusion(bf16[64,512,16]{1,2,0:T(8,128)(2,1)S(1)} %fusion.12, bf16[64,512,16]{1,2,0:T(8,128)(2,1)S(1)} %fusion.13), kind=kLoop, calls=%fused_computation.2 | loop fusion | bytes 4194304 | tf_op jit(solution)/shard_map/convert_element_type | solution.py:31
  6.8 0.0 copy-done.3
  6.8 0.2 convert_reduce_fusion
  7.0 0.1 fusion.9.placing_ref
  7.1 0.2 fusion.7.select_ref
  7.3 91.6 %trak.1 = (f32[64,512]{1,0:T(8,128)S(1)}, f32[256,64]{1,0:T(8,128)S(1)}) custom-call(s32[1]{0:T(128)S(6)} %copy.19.seed_ref, bf16[16,64,512]{2,1,0:T(8,128)(2,1)S(1)} %get-tuple-element.8.train_ref, bf16[16,64,512]{2,1,0:T(8,128)(2,1)S(1)} %get-tuple-element.9.query_ref, bf16[2,256,64]{2,1,0:T(8,128)(2,1)S(1)} %fusion.9.placing_ref, ...), custom_call_target="tpu_custom_call" | custom-call | tf_op jit(solution)/shard_map/trak/pallas_call | solution.py:414
  98.9 0.6 reduce_sum.19
  99.6 0.7 copy.20
  (4 shorter events, 0.0 us)
Async XLA Ops:
  0.6 1.0 copy-start
  0.6 4.3 %copy-start.2 = (bf16[64,64,16]{1,2,0:T(8,128)(2,1)S(1)}, bf16[64,64,16]{1,2,0:T(8,128)(2,1)}, u32[]{:S(2)}) copy-start(bf16[64,64,16]{1,2,0:T(8,128)(2,1)} %param.8) | copy-start | bytes 393220
  0.7 4.3 %copy-start.1 = (bf16[64,64,512]{2,1,0:T(8,128)(2,1)S(1)}, bf16[64,64,512]{2,1,0:T(8,128)(2,1)}, u32[]{:S(2)}) copy-start(bf16[64,64,512]{2,1,0:T(8,128)(2,1)} %param.9) | copy-start | bytes 12582916
  4.9 1.9 %copy-start.3 = (s32[64,1]{0,1:T(1,128)S(1)}, s32[64,1]{0,1:T(1,128)}, u32[]{:S(2)}) copy-start(s32[64,1]{0,1:T(1,128)} %param.10) | copy-start | bytes 772

commit v2 on v0

--- a/solution.py
+++ b/solution.py
@@ -12,7 +12,7 @@
 R = 16
 K = 8192
 L = 64
-BLOCK = 64
+BLOCK = 32
 ROWS = 16
 AHEAD = 2
 
@@ -402,7 +402,7 @@
     examples, width = train.shape[1:]
     n_cols = K // (2 * n_mp)
     cols = n_cols // n_pairs
-    tile_cols = max(cols, min(256, n_cols))
+    tile_cols = max(cols, min(512, n_cols))
     n_tiles = n_cols // tile_cols
     n_rows = n_dp * examples // n_mp
     sums = (n_pairs, examples, n_rows)

time: 99.2 us -> 96.1 us (0.969); the launches traced: 98 us -> 95.9 us
  Pallas kernels: 89.4 us -> 87.3 us
    pallas_call x1, Pallas kernels: 89.4 us -> 87.3 us  [trak(): pl.pallas_call(functools.partial(trak_kernel, n_mp, R * 3 // 4), out_shap...]
where the time goes in v2:
time: 96.1 us; the launch traced here: 95.9 us
  Pallas kernels  87.3 us (91%)
  matrix products  3.99 us (4%)
  local copies, waits for them, and re-layouts  1.97 us (2%)
  between operations  1.55 us (2%)
  other arithmetic  1.12 us (1%)
    pallas_call x1, Pallas kernels, trak(): pl.pallas_call(functools.partial(trak_kernel, n_mp, R * 3 // 4), out_shap...  87.3 us
    dot_general x2, matrix products, local_grads(): jnp.einsum('ntr,ntj->rnj', inputs, out_grads, preferred_element_type=jnp....  3.99 us

profile of v2, /device:TPU:15, one launch (start us, length us, event | category | flops | bytes accessed | tf_op | source)
XLA Modules:
  0.0 95.9 jit_solution(15937809690653482580)
XLA Ops:
  0.6 0.0 copy-start
  0.6 0.0 copy-start.2
  0.7 0.0 copy-start.1
  1.5 0.1 copy-done
  1.6 3.3 %fusion.12 = bf16[64,512,16]{1,2,0:T(8,128)(2,1)S(1)} fusion(bf16[64,64,16]{1,2,0:T(8,128)(2,1)S(1)} %copy-done, bf16[64,64,512]{2,1,0:T(8,128)(2,1)} %param.7), kind=kOutput, calls=%fused_computation.28 | convolution fusion | flops 67108864 | bytes 5373952 | tf_op jit(solution)/shard_map/ntr,ntj->rnj/dot_general | solution.py:31
  4.9 0.0 copy-done.2
  4.9 0.0 copy-done.1
  4.9 0.0 copy-start.3
  5.0 0.7 fusion.13
  5.6 1.2 %fusion = (bf16[16,64,512]{2,1,0:T(8,128)(2,1)S(1)}, bf16[16,64,512]{2,1,0:T(8,128)(2,1)S(1)}) fusion(bf16[64,512,16]{1,2,0:T(8,128)(2,1)S(1)} %fusion.12, bf16[64,512,16]{1,2,0:T(8,128)(2,1)S(1)} %fusion.13), kind=kLoop, calls=%fused_computation.2 | loop fusion | bytes 4194304 | tf_op jit(solution)/shard_map/convert_element_type | solution.py:31
  6.8 0.0 copy-done.3
  6.8 0.2 convert_reduce_fusion
  7.0 0.1 fusion.9.placing_ref
  7.1 0.2 fusion.7.select_ref
  7.3 87.3 %trak.1 = (f32[64,512]{1,0:T(8,128)S(1)}, f32[256,64]{1,0:T(8,128)S(1)}) custom-call(s32[1]{0:T(128)S(6)} %copy.19.seed_ref, bf16[16,64,512]{2,1,0:T(8,128)(2,1)S(1)} %get-tuple-element.8.train_ref, bf16[16,64,512]{2,1,0:T(8,128)(2,1)S(1)} %get-tuple-element.9.query_ref, bf16[2,256,64]{2,1,0:T(8,128)(2,1)S(1)} %fusion.9.placing_ref, ...), custom_call_target="tpu_custom_call" | custom-call | tf_op jit(solution)/shard_map/trak/pallas_call | solution.py:412
  94.6 0.6 reduce_sum.19
  95.3 0.7 copy.20
  (4 shorter events, 0.0 us)
Async XLA Ops:
  0.6 1.0 copy-start
  0.6 4.3 %copy-start.2 = (bf16[64,64,16]{1,2,0:T(8,128)(2,1)S(1)}, bf16[64,64,16]{1,2,0:T(8,128)(2,1)}, u32[]{:S(2)}) copy-start(bf16[64,64,16]{1,2,0:T(8,128)(2,1)} %param.8) | copy-start | bytes 393220
  0.7 4.3 %copy-start.1 = (bf16[64,64,512]{2,1,0:T(8,128)(2,1)S(1)}, bf16[64,64,512]{2,1,0:T(8,128)(2,1)}, u32[]{:S(2)}) copy-start(bf16[64,64,512]{2,1,0:T(8,128)(2,1)} %param.9) | copy-start | bytes 12582916
  4.9 1.9 %copy-start.3 = (s32[64,1]{0,1:T(1,128)S(1)}, s32[64,1]{0,1:T(1,128)}, u32[]{:S(2)}) copy-start(s32[64,1]{0,1:T(1,128)} %param.10) | copy-start | bytes 772
